TPU v7x, 32 devices: a whole 2x2x4 slice. The times are simulated.
32 devices in a mesh: halo: 2 (over x), leaf: 16 (over z, y, core).
Axes of the slice: x: 2, y: 2, z: 4, core: 2. Of those that a mesh axis runs over, the one named last changes fastest.
Arguments:
- start_modes: bfloat16 [16, 128, 8, 4, 128], P('leaf', None, 'halo'), may hold values from -6 to 6
- density: float32 [16, 8, 4, 128], P('leaf', 'halo'), may hold values from 0.5 to 4
- planes: int32 [16], P('leaf'), may hold values from 1 to 8, 75 in all
- tree_order: int32 [16], replicated, may hold values from 0 to 15, each once
- iface_index: int32 [16, 2, 128], P('leaf', None, 'halo'), may hold values from 0 to 2047
- iface_stiff: float32 [16, 2, 128], P('leaf', None, 'halo'), may hold values from 0.5 to 2
- reduced_start: float32 [384, 128], replicated, may hold values from -6 to 6
Outputs:
- modes: float32 [16, 128, 8, 4, 128], P('leaf', None, 'halo')
- reduced: float32 [16, 128, 128], P('leaf')
All inputs are finite; a program needn't handle non-finite values. No bound on the sum of `planes` on one device may be relied on, other than what follows from the above.
Results may differ from a plain program's by a relative error of at most 0.0003.
Values sent between devices are 32-bit elements; how exact they have to be, the bound alone decides.
A program may use at most 64 MiB of HBM per device.

v0:
```python
import functools
import math

import jax
import jax.numpy as jnp
from jax import lax
from jax.experimental import pallas as pl
from jax.experimental.pallas import tpu as pltpu
from jax.sharding import PartitionSpec as P

RITERS = 2
EXACT = lax.Precision.HIGHEST
VMEM_LIMIT = 48 * 1024 * 1024
F32 = jnp.float32


def nn(a, b):
    return lax.dot_general(a, b, (((1,), (0,)), ((), ())), precision=EXACT, preferred_element_type=F32)


def nt(a, b):
    return lax.dot_general(a, b, (((1,), (1,)), ((), ())), precision=EXACT, preferred_element_type=F32)


def lower_inverses(grams):
    n = grams[0].shape[0]
    wide = (8, n)
    row_ids = lax.broadcasted_iota(jnp.int32, wide, 0)
    lane_ids = lax.broadcasted_iota(jnp.int32, wide, 1)
    count = n // 8
    left = [[g[8 * i : 8 * i + 8, :] for i in range(count)] for g in grams]
    right = [[(lane_ids == row_ids + 8 * i).astype(F32) for i in range(count)] for _ in grams]

    def row_of(block, k):
        return jnp.broadcast_to(block[k : k + 1, :], wide)

    def column_of(block, k):
        return jnp.broadcast_to(block[:, k : k + 1], wide)

    for p in range(count):
        for a, b in zip(left, right):
            diag = [column_of(a[p], 8 * p + j) for j in range(8)]
            top_a, top_b = a[p], b[p]
            scales, factors, rows_a, rows_b = [], {}, [], []
            for k in range(8):
                scale = lax.rsqrt(row_of(diag[k], k))
                column = diag[k] * scale
                below = jnp.where(row_ids > k, column, 0.0)
                row_a, row_b = row_of(top_a, k) * scale, row_of(top_b, k) * scale
                top_a = top_a - below * row_a
                top_b = jnp.where(row_ids == k, row_b, top_b - below * row_b)
                for j in range(k + 1, 8):
                    factors[j, k] = row_of(column, j)
                    diag[j] = diag[j] - below * factors[j, k]
                scales.append(scale)
                rows_a.append(row_a)
                rows_b.append(row_b)
            b[p] = top_b
            for i in range(p + 1, count):
                columns = [column_of(a[i], 8 * p + j) for j in range(8)]
                new_a, new_b = a[i], b[i]
                for k in range(8):
                    c = columns[k]
                    for m in range(k):
                        c = c - columns[m] * factors[k, m]
                    columns[k] = c * scales[k]
                    new_a = new_a - columns[k] * rows_a[k]
                    new_b = new_b - columns[k] * rows_b[k]
                a[i], b[i] = new_a, new_b
    return [jnp.concatenate(b, axis=0) for b in right]


def own_kernel(sums_ref, rows_ref, inverse_ref, pack_ref):
    n = sums_ref.shape[1]
    (inverse,) = lower_inverses([sums_ref[0:n, :]])
    inverse_ref[...] = inverse
    pack_ref[0:n, :] = nt(nn(inverse, sums_ref[n : 2 * n, :]), inverse)
    pack_ref[n : 3 * n, :] = nt(rows_ref[...], inverse)


def merge_kernel(
    cells,
    local_cells,
    slot_ref,
    base_ref,
    quad_ref,
    index_row_ref,
    index_col_ref,
    stiff_ref,
    start_ref,
    inverse_ref,
    own_col_ref,
    image_ref,
    modes_ref,
    reduced_ref,
    matrix_ref,
    state_ref,
):
    n = inverse_ref.shape[0]
    coupling = 0.5 * math.sqrt(cells / n)
    eye = lax.broadcasted_iota(jnp.int32, (n, n), 0) == lax.broadcasted_iota(jnp.int32, (n, n), 1)

    def set_matrix(spot, first, second, rows_first, rows_second, stiff):
        m = matrix_ref.at[spot]
        zero = jnp.zeros((n, n), F32)
        m[0:n, 0:n] = first
        m[0:n, n : 2 * n] = zero
        m[n : 2 * n, 0:n] = zero
        m[n : 2 * n, n : 2 * n] = second
        rows_first = coupling * rows_first
        rows_second = coupling * rows_second
        m[0:n, 2 * n : 3 * n] = rows_first.T
        m[n : 2 * n, 2 * n : 3 * n] = rows_second.T
        m[2 * n : 3 * n, 0:n] = rows_first
        m[2 * n : 3 * n, n : 2 * n] = rows_second
        m[2 * n : 3 * n, 2 * n : 3 * n] = jnp.where(eye, jnp.broadcast_to(stiff, (n, n)), 0.0)

    def iterate(spots):
        for spot in spots:
            state_ref[spot] = start_ref[...]

        def step(_, carry):
            products = [nt(state_ref[s], matrix_ref[s]) for s in spots]
            inverses = lower_inverses([nt(p, p) for p in products])
            for s, p, inv in zip(spots, products, inverses):
                state_ref[s] = nn(inv, p)
            return carry

        lax.fori_loop(0, RITERS, step, 0)
        return [nt(state_ref[s], nt(state_ref[s], matrix_ref[s])) for s in spots]

    for pair in range(2):
        a, b = 2 * pair, 2 * pair + 1
        set_matrix(
            pair,
            quad_ref[a, 0:n, :],
            quad_ref[b, 0:n, :],
            quad_ref[a, n : 2 * n, :],
            quad_ref[b, n : 2 * n, :],
            stiff_ref[a, 0:1, :] + stiff_ref[b, 0:1, :],
        )
    reduced = iterate((0, 1))
    half = 1.0 / math.sqrt(2.0)
    merged = []
    for pair in range(2):
        total = None
        faces = state_ref[pair, :, 2 * n : 3 * n]
        for member in range(2):
            t = 2 * pair + member
            match = (index_col_ref[t] == index_row_ref[t]).astype(F32)
            rows = nt(quad_ref[t, 2 * n : 3 * n, :], state_ref[pair, :, member * n : member * n + n])
            rows = rows + half * nt(match, faces)
            total = rows if total is None else total + rows
        merged.append(total)
    stiff = stiff_ref[0, 1:2, :] + stiff_ref[1, 1:2, :] + stiff_ref[2, 1:2, :] + stiff_ref[3, 1:2, :]
    slot = slot_ref[0]
    in_second_pair = slot >= 2
    second_member = (slot == 1) | (slot == 3)
    zero_state = jnp.where(in_second_pair, state_ref[1], state_ref[0])
    zero_own = jnp.where(second_member, zero_state[:, n : 2 * n], zero_state[:, 0:n])
    zero_faces = zero_state[:, 2 * n : 3 * n]
    set_matrix(2, reduced[0], reduced[1], merged[0], merged[1], stiff)
    (final,) = iterate((2,))
    reduced_ref[...] = final
    one_own = jnp.where(in_second_pair, state_ref[2, :, n : 2 * n], state_ref[2, :, 0:n])
    one_faces = state_ref[2, :, 2 * n : 3 * n]
    scale = math.sqrt(cells)
    left = scale * jnp.concatenate(
        [nn(one_own, nn(zero_own, inverse_ref[...])), half * nn(one_own, zero_faces), 0.5 * one_faces], axis=1
    )
    base = base_ref[0]
    for at in range(0, local_cells, 512):
        ids = lax.broadcasted_iota(jnp.int32, (n, 512), 1) + (base + at)
        right = jnp.concatenate(
            [
                image_ref[:, at : at + 512],
                (own_col_ref[0] == ids).astype(F32),
                (own_col_ref[1] == ids).astype(F32),
            ],
            axis=0,
        )
        modes_ref[:, at : at + 512] = nn(left, right)


def vmem():
    return pl.BlockSpec(memory_space=pltpu.VMEM)


def smem():
    return pl.BlockSpec(memory_space=pltpu.SMEM)


def image_kernel(
    halo_count,
    start_ref,
    density_ref,
    planes_ref,
    position_ref,
    small_ref,
    image_ref,
    sums_ref,
    rows_ref,
    small_out_ref,
    first_ref,
    applied_ref,
    from_left,
    from_right,
    density_left,
    density_right,
    parts,
    smalls,
    edge_send,
    edge_recv,
    density_send,
    density_recv,
    part_send,
    part_recv,
    small_send,
    small_recv,
):
    n = start_ref.shape[0]
    lines = density_ref.shape[0]
    extent = lines // 4
    plane = 512
    h = lax.axis_index("halo")
    has_left, has_right = h > 0, h < halo_count - 1
    left, right = lax.rem(h + halo_count - 1, halo_count), lax.rem(h + 1, halo_count)

    barrier = pltpu.get_barrier_semaphore()
    for d in range(1, halo_count):
        peer = lax.rem(h + d, halo_count)
        pl.semaphore_signal(barrier, inc=1, device_id={"halo": peer}, device_id_type=pl.DeviceIdType.MESH)
    pl.semaphore_wait(barrier, halo_count - 1)

    def send(src, dst, send_sem, recv_sem, peer):
        return pltpu.make_async_remote_copy(
            src_ref=src,
            dst_ref=dst,
            send_sem=send_sem,
            recv_sem=recv_sem,
            device_id={"halo": peer},
            device_id_type=pl.DeviceIdType.MESH,
        )

    blocks = [start_ref, first_ref, image_ref, applied_ref]
    last = (extent - 1) * plane

    def to_right(step):
        src = blocks[step].at[:, last : last + plane]
        return send(src, from_left.at[step], edge_send.at[step, 0], edge_recv.at[step, 0], right)

    def to_left(step):
        src = blocks[step].at[:, 0:plane]
        return send(src, from_right.at[step], edge_send.at[step, 1], edge_recv.at[step, 1], left)

    def density_to_right():
        return send(density_ref, density_left, density_send.at[0], density_recv.at[0], right)

    def density_to_left():
        return send(density_ref, density_right, density_send.at[1], density_recv.at[1], left)

    def start_edges(step):
        @pl.when(has_right)
        def _():
            to_right(step).start()

        @pl.when(has_left)
        def _():
            to_left(step).start()

    start_edges(0)

    @pl.when(has_right)
    def _():
        density_to_right().start()

    @pl.when(has_left)
    def _():
        density_to_left().start()

    smalls[h] = small_ref[...]

    def small_copy(d):
        peer = lax.rem(h + d, halo_count)
        return send(smalls.at[h], smalls.at[h], small_send.at[d - 1], small_recv.at[h], peer)

    for d in range(1, halo_count):
        small_copy(d).start()

    @pl.when(jnp.logical_not(has_left))
    def _():
        from_left[...] = jnp.zeros_like(from_left)
        density_left[...] = jnp.zeros_like(density_left)

    @pl.when(jnp.logical_not(has_right))
    def _():
        from_right[...] = jnp.zeros_like(from_right)
        density_right[...] = jnp.zeros_like(density_right)

    mask = [
        jnp.where(h * extent + x < planes_ref[0], jnp.float32(1.0), jnp.float32(0.0)) for x in range(-1, extent + 1)
    ]
    chunk = 32
    lane = lax.broadcasted_iota(jnp.int32, (chunk, 128), 1)

    def smooth(values):
        lower = jnp.where(lane == 0, 0.0, pltpu.roll(values, 1, 1))
        upper = jnp.where(lane == 127, 0.0, pltpu.roll(values, 127, 1))
        return 0.5 * lower + values + 0.5 * upper

    def apply_plane(step, x):
        block, out = blocks[step], blocks[step + 1]

        def body(c, carry):
            here = pl.ds(pl.multiple_of(c * chunk, chunk), chunk)
            sums_a, sums_b = [], []
            for y in range(4):
                at = y * 128
                total_a = total_b = None
                for near in (x - 1, x, x + 1):
                    if near < 0:
                        u = from_left[step, here, at : at + 128]
                        rho = density_left[lines - 4 + y : lines - 3 + y, :]
                    elif near == extent:
                        u = from_right[step, here, at : at + 128]
                        rho = density_right[y : y + 1, :]
                    else:
                        u = block[here, near * plane + at : near * plane + at + 128]
                        rho = density_ref[4 * near + y : 4 * near + y + 1, :]
                    weight = mask[near + 1] if near == x else 0.5 * mask[near + 1]
                    u = weight * u
                    v = u * rho
                    total_a = u if total_a is None else total_a + u
                    total_b = v if total_b is None else total_b + v
                sums_a.append(total_a)
                sums_b.append(total_b)
            for y in range(4):
                a, b = sums_a[y], sums_b[y]
                for other in (y - 1, y + 1):
                    if 0 <= other < 4:
                        a = a + 0.5 * sums_a[other]
                        b = b + 0.5 * sums_b[other]
                rho = density_ref[4 * x + y : 4 * x + y + 1, :]
                at = x * plane + y * 128
                out[here, at : at + 128] = (mask[x + 1] * 0.0625) * (rho * smooth(a) + smooth(b))
            return carry

        lax.fori_loop(0, n // chunk, body, 0)

    for step in range(3):
        if step > 0:
            start_edges(step)
        for x in range(1, extent - 1):
            apply_plane(step, x)

        @pl.when(has_right)
        def _():
            to_left(step).wait_recv()

        @pl.when(has_left)
        def _():
            to_right(step).wait_recv()

        if step == 0:

            @pl.when(has_right)
            def _():
                density_to_left().wait_recv()

            @pl.when(has_left)
            def _():
                density_to_right().wait_recv()

        apply_plane(step, 0)
        apply_plane(step, extent - 1)

    faces = position_ref.shape[0]
    cells = image_ref.shape[1]
    image = image_ref[...]
    ids = lax.broadcasted_iota(jnp.int32, (faces, cells), 1)
    match = (position_ref[...] == ids).astype(F32)
    parts[h, 0:n, :] = nt(image, image)
    parts[h, n : 2 * n, :] = nt(image, applied_ref[...])
    parts[h, 2 * n : 2 * n + faces, :] = nt(match, image)

    def part_copy(d):
        peer = lax.rem(h + d, halo_count)
        return send(parts.at[h], parts.at[h], part_send.at[d - 1], part_recv.at[h], peer)

    for d in range(1, halo_count):
        part_copy(d).start()
    for d in range(1, halo_count):
        peer = lax.rem(h + d, halo_count)
        send(parts.at[peer], parts.at[peer], part_send.at[d - 1], part_recv.at[peer], peer).wait_recv()
        send(smalls.at[peer], smalls.at[peer], small_send.at[d - 1], small_recv.at[peer], peer).wait_recv()
    total = parts[0, 0 : 2 * n, :]
    for j in range(1, halo_count):
        total = total + parts[j, 0 : 2 * n, :]
    sums_ref[...] = total
    half = faces // 2
    for j in range(halo_count):
        for level in range(2):
            at = level * n + j * half
            rows_ref[at : at + half, :] = parts[j, 2 * n + level * half : 2 * n + (level + 1) * half, :]
    small_out_ref[...] = smalls[...]

    for step in range(3):

        @pl.when(has_right)
        def _():
            to_right(step).wait_send()

        @pl.when(has_left)
        def _():
            to_left(step).wait_send()

    @pl.when(has_right)
    def _():
        density_to_right().wait_send()

    @pl.when(has_left)
    def _():
        density_to_left().wait_send()

    for d in range(1, halo_count):
        small_copy(d).wait_send()
        part_copy(d).wait_send()


def image_phase(start_modes, density, planes, positions, small):
    n = start_modes.shape[1]
    extent = start_modes.shape[2]
    cells = extent * start_modes.shape[3] * start_modes.shape[4]
    count = lax.axis_size("halo")
    faces = positions.size
    small = jnp.pad(small, ((0, 8 - small.shape[0]), (0, 128 - small.shape[1])))
    dma = pltpu.SemaphoreType.DMA
    image, sums, rows, smalls = pl.pallas_call(
        functools.partial(image_kernel, count),
        out_shape=(
            jax.ShapeDtypeStruct((n, cells), F32),
            jax.ShapeDtypeStruct((2 * n, n), F32),
            jax.ShapeDtypeStruct((2 * n, n), F32),
            jax.ShapeDtypeStruct((count, 8, 128), F32),
        ),
        in_specs=[vmem(), vmem(), smem(), vmem(), vmem()],
        out_specs=(vmem(),) * 4,
        scratch_shapes=[
            pltpu.VMEM((n, cells), F32),
            pltpu.VMEM((n, cells), F32),
            pltpu.VMEM((3, n, 512), F32),
            pltpu.VMEM((3, n, 512), F32),
            pltpu.VMEM((4 * extent, 128), F32),
            pltpu.VMEM((4 * extent, 128), F32),
            pltpu.VMEM((count, 2 * n + faces, n), F32),
            pltpu.VMEM((count, 8, 128), F32),
            dma((3, 2)),
            dma((3, 2)),
            dma((2,)),
            dma((2,)),
            dma((count - 1,)),
            dma((count,)),
            dma((count - 1,)),
            dma((count,)),
        ],
        compiler_params=pltpu.CompilerParams(
            collective_id=0, has_side_effects=True, vmem_limit_bytes=VMEM_LIMIT
        ),
        name="image_phase",
    )(
        start_modes[0].astype(F32).reshape(n, cells),
        density[0].reshape(4 * extent, 128),
        planes,
        positions.reshape(faces, 1),
        small,
    )
    return image, sums, rows, smalls


def per_device(start_modes, density, planes, tree_order, iface_index, iface_stiff, reduced_start):
    n = start_modes.shape[1]
    block_shape = start_modes.shape[1:]
    local_cells = start_modes.shape[2] * start_modes.shape[3] * start_modes.shape[4]
    halo_index = lax.axis_index("halo")
    leaf_size = lax.axis_size("leaf")
    leaf_index = lax.axis_index("leaf")
    cells = local_cells * lax.axis_size("halo")
    base = halo_index * local_cells

    leaf_ids = jnp.arange(leaf_size, dtype=jnp.int32)
    pair_of = tree_order // 2
    quad_mask = tree_order // 4 == tree_order[leaf_index] // 4
    a0 = jnp.min(jnp.where(quad_mask, leaf_ids, leaf_size))
    first_pair = pair_of == tree_order[a0] // 2
    second_pair = quad_mask & ~first_pair
    b0 = jnp.max(jnp.where(first_pair, leaf_ids, -1))
    a1 = jnp.min(jnp.where(second_pair, leaf_ids, leaf_size))
    b1 = jnp.max(jnp.where(second_pair, leaf_ids, -1))
    members = jnp.stack([a0, b0, a1, b1])
    slot = jnp.sum(jnp.where(members == leaf_index, jnp.arange(4, dtype=jnp.int32), 0))

    small = jnp.concatenate([iface_stiff[0], (iface_index[0] + base).astype(F32)], axis=0)
    image, sums, rows, smalls = image_phase(start_modes, density, planes, iface_index[0], small)
    small = smalls[:, :, : iface_index.shape[2]].transpose(1, 0, 2).reshape(8, n)
    inverse, pack = pl.pallas_call(
        own_kernel,
        out_shape=(jax.ShapeDtypeStruct((n, n), F32), jax.ShapeDtypeStruct((3 * n, n), F32)),
        in_specs=[vmem()] * 2,
        out_specs=(vmem(), vmem()),
        compiler_params=pltpu.CompilerParams(vmem_limit_bytes=VMEM_LIMIT),
        name="own_problem",
    )(sums, rows)
    full = jnp.concatenate([pack, small], axis=0)
    gathered = lax.all_gather(full[None], "leaf", axis=0, tiled=True)
    quad = jnp.take(gathered, members, axis=0)
    quad_small = quad[:, 3 * n :, :]
    stiff = quad_small[:, 0:2, :]
    index_row = quad_small[:, 2:3, :]
    index_col = quad_small[:, 3, :, None]
    own_col = small[2:4, :, None].astype(jnp.int32)
    modes, reduced = pl.pallas_call(
        functools.partial(merge_kernel, cells, local_cells),
        out_shape=(jax.ShapeDtypeStruct((n, local_cells), F32), jax.ShapeDtypeStruct((n, n), F32)),
        in_specs=[smem()] * 2 + [vmem()] * 8,
        out_specs=(vmem(), vmem()),
        scratch_shapes=[pltpu.VMEM((3, 3 * n, 3 * n), F32), pltpu.VMEM((3, n, 3 * n), F32)],
        compiler_params=pltpu.CompilerParams(vmem_limit_bytes=VMEM_LIMIT),
        name="merge_problems",
    )(
        slot[None],
        base[None].astype(jnp.int32),
        quad,
        index_row,
        index_col,
        stiff,
        reduced_start.T,
        inverse,
        own_col,
        image,
    )
    return modes.reshape((1,) + tuple(block_shape)), reduced[None]


def solution(mesh):
    return jax.shard_map(
        per_device,
        mesh=mesh,
        in_specs=(
            P("leaf", None, "halo", None, None),
            P("leaf", "halo", None, None),
            P("leaf"),
            P(),
            P("leaf", None, "halo"),
            P("leaf", None, "halo"),
            P(),
        ),
        out_specs=(P("leaf", None, "halo", None, None), P("leaf", None, None)),
        check_vma=False,
    )
```

profile of v0, /device:TPU:0, one launch (start us, length us, event | category | flops | bytes accessed | tf_op | source)
XLA Modules:
  0.0 142.5 jit_solution(2718178452178224556)
XLA Ops:
  7.2 0.0 copy-start.4
  7.2 0.0 copy-start.3
  7.2 0.0 all-gather.3.cloned.1.call-start
  7.2 1.3 reshape.215.start_ref
  9.2 0.8 reshape_squeeze.8.position_ref
  10.1 0.7 convert_bitcast_fusion
  10.7 0.7 select_maximum_fusion.small_ref
  11.4 0.7 copy-done.2
  12.1 33.6 %image_phase.1 = (f32[128,2048]{1,0:T(8,128)S(1)}, f32[256,128]{1,0:T(8,128)S(1)}, f32[256,128]{1,0:T(8,128)S(1)}, f32[2,8,128]{2,1,0:T(8,128)S(1)}) custom-call(f32[128,2048]{1,0:T(8,128)S(1)} %reshape.215.start_ref, f32[16,128]{1,0:T(8,128)S(1)} %bitcast.25, s32[1]{0:T(128)S(6)} %copy.20.planes_ref, s32[128,1]{1,0:T(8,128)S(1)} %reshape_squeeze.8.position_ref, ...), custom_call_target="tpu_custom_call" | custom-call | tf_op jit(solution)/shard_map/image_phase/pallas_call | solution.py:438
  45.7 0.1 reshape.213
  45.8 4.5 %own_problem.1 = (f32[128,128]{1,0:T(8,128)S(1)}, f32[384,128]{1,0:T(8,128)S(1)}) custom-call(f32[256,128]{1,0:T(8,128)S(1)} %get-tuple-element.10.sums_ref, f32[256,128]{1,0:T(8,128)S(1)} %get-tuple-element.11.rows_ref), custom_call_target="tpu_custom_call" | custom-call | tf_op jit(solution)/shard_map/own_problem/pallas_call | solution.py:505
  50.4 0.0 copy-start
  50.4 0.7 pad_maximum_fusion
  51.1 0.0 all-gather.3.cloned.1.call-update
  51.1 0.6 dynamic_slice.6
  54.0 0.6 fusion
  56.3 0.6 dynamic_slice.7
  59.1 0.1 copy.16
  59.3 0.1 convert_element_type.27.own_col_ref
  59.4 0.6 fusion.1
  60.1 0.7 select_reduce_fusion.1
  60.8 2.5 %fusion.3 = s32[4]{0:T(128)S(1)} fusion(s32[1,1]{0,1:T(1,128)} %bitcast.16, s32[1,1]{0,1:T(1,128)} %bitcast.15, s32[1,1]{0,1:T(1,128)} %bitcast.14, s32[1,1]{0,1:T(1,128)} %bitcast.13), kind=kLoop, calls=%fused_computation.27 | loop fusion | flops 24 | bytes 32 | tf_op jit(solution)/shard_map/jit(_take)/jit(_where)/select_n | solution.py:515
  63.2 2.5 %compare_and_fusion = (pred[4]{0:T(512)(128)(4,1)S(1)}, s32[4]{0:T(128)S(1)}) fusion(s32[1]{0:T(128)} %bitcast.5, s32[1]{0:T(128)} %bitcast.4, s32[1]{0:T(128)} %bitcast.3, s32[1]{0:T(128)} %bitcast.1), kind=kLoop, calls=%fused_computation.11 | loop fusion | flops 36 | bytes 36 | tf_op jit(solution)/shard_map/jit(_take)/and | solution.py:515
  65.7 0.6 fusion.2
  66.3 31.0 %all-gather.3.cloned.1.call-done = f32[6272,128]{1,0:T(8,128)} async-done(((f32[392,128]{1,0:T(8,128)}), f32[6272,128]{1,0:T(8,128)}) %all-gather.3.cloned.1.call-update) | async-done | bytes 3211280 | tf_op jit(solution)/shard_map/all_gather | solution.py:514
  97.4 2.5 %gather_fusion = f32[4,392,128]{2,1,0:T(8,128)S(1)} fusion(f32[16,392,128]{2,1,0:T(8,128)} %bitcast.26, s32[1024]{0:T(1024)S(1)} %pad_clamp_fusion), kind=kCustom, calls=%fused_computation | custom fusion | bytes 1605648 | tf_op jit(solution)/shard_map/jit(_take)/gather | solution.py:515
  99.9 0.1 broadcast_select_fusion.quad_ref
  100.0 0.1 copy.18.index_col_ref
  100.2 0.0 copy-start.1
  100.2 0.8 copy-done.1
  101.0 32.9 %merge_problems.1 = (f32[128,2048]{1,0:T(8,128)S(1)}, f32[128,128]{1,0:T(8,128)}) custom-call(s32[1]{0:T(128)} %bitcast.6.slot_ref, s32[1]{0:T(128)} %bitcast.7.base_ref, f32[4,392,128]{2,1,0:T(8,128)S(1)} %broadcast_select_fusion.quad_ref, f32[4,1,128]{2,1,0:T(1,128)S(1)} %get-tuple-element.27.index_row_ref, f32[4,128,1]{2,1,0:T(8,128)S(1)} %copy.18.index_col_ref, ...), custom_call_target="tpu_custom_call" | custom-call | tf_op jit(solution)/shard_map/merge_problems/pallas_call | solution.py:521
  133.9 1.7 %reshape.214 = f32[1,128,4,4,128]{4,3,2,1,0:T(4,128)} reshape(f32[128,2048]{1,0:T(8,128)S(1)} %get-tuple-element.16) | data formatting | bytes 2097152 | tf_op jit(solution)/shard_map/reshape | solution.py:541
  (11 shorter events, 0.0 us)
Async XLA Ops:
  7.2 43.9 %copy-start.4 = (s32[16]{0:T(128)S(1)}, s32[16]{0:T(128)}, u32[]{:S(2)}) copy-start(s32[16]{0:T(128)} %param.10) | copy-start | bytes 196
  7.2 52.0 %copy-start.3 = (f32[384,128]{1,0:T(8,128)S(1)}, f32[384,128]{1,0:T(8,128)}, u32[]{:S(2)}) copy-start(f32[384,128]{1,0:T(8,128)} %param.13) | copy-start | bytes 589828
  7.2 90.2 %all-gather.3.cloned.1.call-start = ((), (), s32[]{:S(2)}) async-start(), calls=%async_computation | async-start | bytes 3411968 | tf_op jit(solution)/shard_map/all_gather | solution.py:514
  11.4 0.7 copy-start.2
  50.4 49.8 %copy-start = (f32[128,128]{1,0:T(8,128)}, f32[128,128]{1,0:T(8,128)S(1)}, u32[]{:S(2)}) copy-start(f32[128,128]{1,0:T(8,128)S(1)} %get-tuple-element.14.inverse_ref) | copy-start | bytes 196612
  100.2 0.8 copy-start.1
Sparse Core Ops, SparseCore 0:
  51.2 46.1 all-gather.2
where the time goes:
time: 143 us; the launch traced here: 142 us
  Pallas kernels  71 us (50%)
  waiting for transfers between devices  31.1 us (22%)
  between operations  21.1 us (15%)
  other arithmetic  9.73 us (7%)
  local copies, waits for them, and re-layouts  9.57 us (7%)
    pallas_call x1, Pallas kernels, image_phase(): pl.pallas_call(functools.partial(image_kernel, count), out_shape=(jax.Sha...  33.6 us
    pallas_call x1, Pallas kernels, per_device(): pl.pallas_call(functools.partial(merge_kernel, cells, local_cells), out_s...  32.9 us
    all_gather x1, waiting for transfers between devices, per_device(): gathered = lax.all_gather(full[None], 'leaf', axis=0, tiled=True)  31 us
    pallas_call x1, Pallas kernels, per_device(): pl.pallas_call(own_kernel, out_shape=(jax.ShapeDtypeStruct((n, n), F32),...  4.55 us
  transfers between devices with their start and end apart: 1, of which 1 were waited for; matrix products, arithmetic and copies ran while one was open for 6% of the time, Pallas kernels for 0%

commit v1 on v0

--- a/solution.py
+++ b/solution.py
@@ -511,8 +511,12 @@
         name="own_problem",
     )(sums, rows)
     full = jnp.concatenate([pack, small], axis=0)
-    gathered = lax.all_gather(full[None], "leaf", axis=0, tiled=True)
-    quad = jnp.take(gathered, members, axis=0)
+    halo_size = lax.axis_size("halo")
+    share = -(-full.shape[0] // (8 * halo_size)) * 8
+    full = jnp.pad(full, ((0, share * halo_size - full.shape[0]), (0, 0)))
+    piece = lax.dynamic_slice_in_dim(full, halo_index * share, share, 0)
+    gathered = lax.all_gather(piece[None], "leaf", axis=0, tiled=True)
+    quad = lax.all_gather(jnp.take(gathered, members, axis=0), "halo", axis=1, tiled=True)
     quad_small = quad[:, 3 * n :, :]
     stiff = quad_small[:, 0:2, :]
     index_row = quad_small[:, 2:3, :]

time: 143 us -> 148 us (1.035)
  blocking collectives: 0 us -> 12.5 us
  waiting for transfers between devices: 31.1 us -> 23.7 us
    all_gather x0 -> x1, blocking collectives: none -> 12.5 us  [per_device(): lax.all_gather(jnp.take(gathered, members, axis=0), 'halo', axis=1, tiled...]
    all_gather x1, waiting for transfers between devices: 31 us -> 23.6 us  [per_device(): gathered = lax.all_gather(piece[None], 'leaf', axis=0, tiled=True)]
where the time goes in v1:
time: 148 us; the launch traced here: 147 us
  Pallas kernels  71 us (48%)
  waiting for transfers between devices  23.7 us (16%)
  between operations  22.1 us (15%)
  blocking collectives  12.5 us (8%)
  other arithmetic  9.44 us (6%)
  local copies, waits for them, and re-layouts  8.48 us (6%)
    pallas_call x1, Pallas kernels, image_phase(): pl.pallas_call(functools.partial(image_kernel, count), out_shape=(jax.Sha...  33.6 us
    pallas_call x1, Pallas kernels, per_device(): pl.pallas_call(functools.partial(merge_kernel, cells, local_cells), out_s...  32.8 us
    all_gather x1, waiting for transfers between devices, per_device(): gathered = lax.all_gather(piece[None], 'leaf', axis=0, tiled=True)  23.6 us
    all_gather x1, blocking collectives, per_device(): lax.all_gather(jnp.take(gathered, members, axis=0), 'halo', axis=1, tiled...  12.5 us
    pallas_call x1, Pallas kernels, per_device(): pl.pallas_call(own_kernel, out_shape=(jax.ShapeDtypeStruct((n, n), F32),...  4.54 us
  transfers between devices with their start and end apart: 1, of which 1 were waited for; matrix products, arithmetic and copies ran while one was open for 6% of the time, Pallas kernels for 0%

profile of v1, /device:TPU:0, one launch (start us, length us, event | category | flops | bytes accessed | tf_op | source)
XLA Modules:
  0.0 147.1 jit_solution(13928306800299757090)
XLA Ops:
  7.2 0.0 copy-start.5
  7.2 0.0 copy-start.2
  7.2 0.0 all-gather.3.cloned.1.call-start
  7.9 0.8 reshape_squeeze.8.position_ref
  8.7 0.7 convert_bitcast_fusion
  9.4 1.3 reshape.215.start_ref
  10.7 0.0 copy-done.5
  10.8 33.6 %image_phase.1 = (f32[128,2048]{1,0:T(8,128)S(1)}, f32[256,128]{1,0:T(8,128)S(1)}, f32[256,128]{1,0:T(8,128)S(1)}, f32[2,8,128]{2,1,0:T(8,128)S(1)}) custom-call(f32[128,2048]{1,0:T(8,128)S(1)} %reshape.215.start_ref, f32[16,128]{1,0:T(8,128)S(1)} %bitcast.25, s32[1]{0:T(128)S(6)} %copy.20.planes_ref, s32[128,1]{1,0:T(8,128)S(1)} %reshape_squeeze.8.position_ref, ...), custom_call_target="tpu_custom_call" | custom-call | tf_op jit(solution)/shard_map/image_phase/pallas_call | solution.py:438
  44.4 0.1 reshape.213
  44.5 4.5 %own_problem.1 = (f32[128,128]{1,0:T(8,128)S(1)}, f32[384,128]{1,0:T(8,128)S(1)}) custom-call(f32[256,128]{1,0:T(8,128)S(1)} %get-tuple-element.10.sums_ref, f32[256,128]{1,0:T(8,128)S(1)} %get-tuple-element.11.rows_ref), custom_call_target="tpu_custom_call" | custom-call | tf_op jit(solution)/shard_map/own_problem/pallas_call | solution.py:505
  49.1 0.0 copy-start
  49.1 0.7 fusion.1
  49.8 0.0 all-gather.3.cloned.1.call-update
  49.8 0.6 dynamic_slice.9
  53.0 0.7 fusion.3
  55.5 0.7 dynamic_slice.10
  58.9 0.1 copy.16
  59.1 0.1 convert_element_type.29.own_col_ref
  59.2 0.7 fusion.4
  59.9 0.7 select_reduce_fusion.1
  60.6 2.6 %fusion.6 = s32[4]{0:T(128)S(1)} fusion(s32[1,1]{0,1:T(1,128)} %bitcast.16, s32[1,1]{0,1:T(1,128)} %bitcast.15, s32[1,1]{0,1:T(1,128)} %bitcast.14, s32[1,1]{0,1:T(1,128)} %bitcast.13), kind=kLoop, calls=%fused_computation.32 | loop fusion | flops 24 | bytes 32 | tf_op jit(solution)/shard_map/jit(_take)/jit(_where)/select_n | solution.py:519
  63.2 2.6 %compare_and_fusion = (pred[4]{0:T(512)(128)(4,1)S(1)}, s32[4]{0:T(128)S(1)}) fusion(s32[1]{0:T(128)} %bitcast.5, s32[1]{0:T(128)} %bitcast.4, s32[1]{0:T(128)} %bitcast.3, s32[1]{0:T(128)} %bitcast.1), kind=kLoop, calls=%fused_computation.16 | loop fusion | flops 36 | bytes 36 | tf_op jit(solution)/shard_map/jit(_take)/and | solution.py:519
  65.9 0.7 fusion.5
  66.5 23.6 %all-gather.3.cloned.1.call-done = f32[3200,128]{1,0:T(8,128)} async-done(((f32[200,128]{1,0:T(8,128)}), f32[3200,128]{1,0:T(8,128)}) %all-gather.3.cloned.1.call-update) | async-done | bytes 1638416 | tf_op jit(solution)/shard_map/all_gather | solution.py:518
  90.2 2.0 %gather_fusion = f32[4,200,128]{2,1,0:T(8,128)S(1)} fusion(f32[16,200,128]{2,1,0:T(8,128)} %bitcast.26, s32[1024]{0:T(1024)S(1)} %pad_clamp_fusion), kind=kCustom, calls=%fused_computation | custom fusion | bytes 819216 | tf_op jit(solution)/shard_map/jit(_take)/gather | solution.py:519
  92.2 0.1 broadcast_select_fusion
  92.3 12.5 %all_gather.7.quad_ref = f32[4,400,128]{2,1,0:T(8,128)S(1)} all-gather(f32[4,200,128]{2,1,0:T(8,128)S(1)} %broadcast_select_fusion), channel_id=1, replica_groups=mesh['halo'=2,'leaf'=16] {'halo'}, dimensions={1}, use_global_device_ids=true | all-gather | bytes 1228800 | tf_op jit(solution)/shard_map/all_gather | solution.py:519
  104.8 0.1 copy.18.index_col_ref
  104.9 0.0 copy-start.1
  105.0 0.8 copy-done.1
  105.8 32.8 %merge_problems.1 = (f32[128,2048]{1,0:T(8,128)S(1)}, f32[128,128]{1,0:T(8,128)}) custom-call(s32[1]{0:T(128)} %bitcast.6.slot_ref, s32[1]{0:T(128)} %bitcast.7.base_ref, f32[4,400,128]{2,1,0:T(8,128)S(1)} %all_gather.7.quad_ref, f32[4,1,128]{2,1,0:T(1,128)S(1)} %get-tuple-element.27.index_row_ref, f32[4,128,1]{2,1,0:T(8,128)S(1)} %copy.18.index_col_ref, ...), custom_call_target="tpu_custom_call" | custom-call | tf_op jit(solution)/shard_map/merge_problems/pallas_call | solution.py:525
  138.6 1.7 %reshape.214 = f32[1,128,4,4,128]{4,3,2,1,0:T(4,128)} reshape(f32[128,2048]{1,0:T(8,128)S(1)} %get-tuple-element.16) | data formatting | bytes 2097152 | tf_op jit(solution)/shard_map/reshape | solution.py:545
  (14 shorter events, 0.1 us)
Async XLA Ops:
  7.2 3.6 %copy-start.5 = (f32[1,2,64]{2,1,0:T(2,128)S(1)}, f32[1,2,64]{2,1,0:T(2,128)}, u32[]{:S(2)}) copy-start(f32[1,2,64]{2,1,0:T(2,128)} %param.12) | copy-start | bytes 1540
  7.2 3.6 %copy-start.2 = (f32[1,4,4,128]{3,2,1,0:T(4,128)S(1)}, f32[1,4,4,128]{3,2,1,0:T(4,128)}, u32[]{:S(2)}) copy-start(f32[1,4,4,128]{3,2,1,0:T(4,128)} %param.8) | copy-start | bytes 24580
  7.2 83.0 %all-gather.3.cloned.1.call-start = ((), (), s32[]{:S(2)}) async-start(), calls=%async_computation | async-start | bytes 1740800 | tf_op jit(solution)/shard_map/all_gather | solution.py:518
  9.4 40.4 %copy-start.4 = (s32[16]{0:T(128)S(1)}, s32[16]{0:T(128)}, u32[]{:S(2)}) copy-start(s32[16]{0:T(128)} %param.10) | copy-start | bytes 196
  9.4 49.5 %copy-start.3 = (f32[384,128]{1,0:T(8,128)S(1)}, f32[384,128]{1,0:T(8,128)}, u32[]{:S(2)}) copy-start(f32[384,128]{1,0:T(8,128)} %param.13) | copy-start | bytes 589828
  49.1 55.7 %copy-start = (f32[128,128]{1,0:T(8,128)}, f32[128,128]{1,0:T(8,128)S(1)}, u32[]{:S(2)}) copy-start(f32[128,128]{1,0:T(8,128)S(1)} %get-tuple-element.14.inverse_ref) | copy-start | bytes 196612
  104.9 0.8 copy-start.1
Sparse Core Ops, SparseCore 0:
  49.9 40.2 all-gather.2
